TPU v7x, 32 devices: a whole 2x2x4 slice. The times are simulated.
32 devices in a mesh: seed: 4 (over z), tok: 8 (over y, x, core).
Axes of the slice: x: 2, y: 2, z: 4, core: 2. Of those that a mesh axis runs over, the one named last changes fastest.
Arguments:
- atom_single: bfloat16 [8192, 128], P(('seed', 'tok')), parts along dimension 0, may hold values from -6 to 6
- atom_bias: bfloat16 [2048, 512], P('tok'), may hold values from -400 to 400
- atom_token: int32 [2048], P('tok'), may hold values from 0 to 255, as said below
- atom_counts: int32 [256], P('tok'), may hold values from 1 to 15, as said below
- pair_rep: bfloat16 [256, 256, 128], P('tok'), may hold values from -400 to 400
- atom_qkv_w: bfloat16 [128, 384], replicated, may hold values from -0.5 to 0.5
- atom_out_w: bfloat16 [128, 128], replicated, may hold values from -0.5 to 0.5
- agg_w: bfloat16 [128, 768], replicated, may hold values from -0.5 to 0.5
- tok_qkv_w: bfloat16 [2, 768, 2304], replicated, may hold values from -0.21875 to 0.21875
- tok_out_w: bfloat16 [2, 768, 768], replicated, may hold values from -0.4375 to 0.4375
- pair_w: bfloat16 [128, 32], replicated, may hold values from -0.5 to 0.5
- bcast_w: bfloat16 [768, 128], replicated, may hold values from -0.21875 to 0.21875
Outputs:
- atom_out: bfloat16 [8192, 128], P(('seed', 'tok')), parts along dimension 0
- token_out: bfloat16 [1024, 768], P(('seed', 'tok')), parts along dimension 0
There are 4 independent parts, one for each index of `seed`. A program takes and returns all parts, laid end to end along the dimension named above; an argument that names none is the same for every part. Nothing has to cross between parts.
Inputs may be any that keep to these rules, and one draw needn't show every extreme that they name: `atom_counts`: counts sum to 2048; the counts of the tokens of one index of tok sum to 256; the largest count is 15 and the smallest 1 in every draw. `atom_token`: token t holds exactly atom_counts[t] atoms, and the atoms of one token are consecutive. Along the atoms the tokens come in increasing order, except that at each boundary between neighbouring indices of tok the first token of the upper index comes just before the last token of the lower index; so every atom belongs to a token of its own index of tok or of a neighbouring one.
All inputs are finite; a program needn't handle non-finite values.
Results may differ from a plain program's by a relative error of at most 0.017.
Values may be sent and summed in bfloat16 or wider, within the bound.
A program may use at most 128 MiB of HBM per device.

v0:
```python
import jax
import jax.numpy as jnp
from jax import lax
from jax.sharding import PartitionSpec as P

C = 768
H = 16
CA = 128
AH = 4
QW = 32
KW = 128
NB = 2
HALO = 48


def with_halo(cells, sides, width):
    for axis, dim in sides:
        count = lax.axis_size(axis)
        ends = count - 1
        head = lax.slice_in_dim(cells, 0, width, axis=dim)
        tail = lax.slice_in_dim(cells, cells.shape[dim] - width, cells.shape[dim], axis=dim)
        cells = jnp.concatenate(
            [
                lax.ppermute(tail, axis, [(i, (i + 1) % count) for i in range(ends)]),
                cells,
                lax.ppermute(head, axis, [((i + 1) % count, i) for i in range(ends)]),
            ],
            axis=dim,
        )
    return cells


def layer_norm(values):
    average = jnp.mean(values, axis=-1, keepdims=True)
    centred = values - average
    variance = jnp.mean(centred * centred, axis=-1, keepdims=True)
    return centred * lax.rsqrt(variance + 1e-05)


def window_attend(queries, keyvals, atom_bias, first_atom, atom_total):
    windows = keyvals.shape[0]
    head_width = CA // AH
    query_heads = queries.reshape(windows, QW, AH, head_width)
    key_heads = keyvals[:, :, :CA].reshape(windows, KW, AH, head_width)
    value_heads = keyvals[:, :, CA:].reshape(windows, KW, AH, head_width)
    scores = jnp.einsum(
        "wqhd,wkhd->whqk", query_heads, key_heads, preferred_element_type=jnp.float32
    ) * head_width ** (-0.5)
    scores = scores + atom_bias.reshape(windows, QW, AH, KW).transpose(0, 2, 1, 3).astype(
        jnp.float32
    )
    position = (
        first_atom
        + QW * jnp.arange(windows, dtype=jnp.int32)[:, None]
        - HALO
        + jnp.arange(KW, dtype=jnp.int32)[None, :]
    )
    inside = (position >= 0) & (position < atom_total)
    scores = jnp.where(inside[:, None, None, :], scores, -1000000000.0)
    maximum = jnp.max(scores, axis=-1, keepdims=True)
    powers = jnp.exp(scores - maximum)
    denominator = jnp.sum(powers, axis=-1)
    weights = powers.astype(jnp.bfloat16)
    mixed_heads = jnp.einsum(
        "whqk,wkhd->wqhd", weights, value_heads, preferred_element_type=jnp.float32
    )
    mixed_heads = mixed_heads / denominator.transpose(0, 2, 1)[..., None]
    return mixed_heads.reshape(windows * QW, CA).astype(jnp.bfloat16)


def member_product(member, lifted):
    upper = lifted.astype(jnp.bfloat16)
    lower = (lifted - upper.astype(jnp.float32)).astype(jnp.bfloat16)
    picker = member.astype(jnp.bfloat16)
    total = jnp.dot(picker, upper, preferred_element_type=jnp.float32)
    return total + jnp.dot(picker, lower, preferred_element_type=jnp.float32)


def local(
    atom_single,
    atom_bias,
    atom_token,
    atom_counts,
    pair_rep,
    atom_qkv_w,
    atom_out_w,
    agg_w,
    tok_qkv_w,
    tok_out_w,
    pair_w,
    bcast_w,
):
    local_atoms = atom_single.shape[0]
    local_tokens = atom_counts.shape[0]
    first_atom = lax.axis_index("tok") * local_atoms
    first_token = lax.axis_index("tok") * local_tokens
    hidden_in = atom_single.astype(jnp.float32)
    normed = layer_norm(hidden_in).astype(jnp.bfloat16)
    projected = jnp.dot(normed, atom_qkv_w, preferred_element_type=jnp.float32).astype(jnp.bfloat16)
    queries = projected[:, :CA]
    padded = with_halo(projected[:, CA:], (("tok", 0),), HALO)
    windows = local_atoms // QW
    gather_index = (
        QW * jnp.arange(windows, dtype=jnp.int32)[:, None]
        + jnp.arange(KW, dtype=jnp.int32)[None, :]
    )
    keyvals = padded[gather_index]
    attended = window_attend(
        queries, keyvals, atom_bias, first_atom, local_atoms * lax.axis_size("tok")
    )
    atom_hidden = (
        hidden_in + jnp.dot(attended, atom_out_w, preferred_element_type=jnp.float32)
    ).astype(jnp.bfloat16)
    lifted = jax.nn.relu(jnp.dot(atom_hidden, agg_w, preferred_element_type=jnp.float32))
    wanted = first_token - local_tokens + jnp.arange(3 * local_tokens, dtype=jnp.int32)
    member = atom_token[None, :] == wanted[:, None]
    partial_sums = member_product(member, lifted)
    outward = jnp.concatenate(
        [partial_sums[:local_tokens], partial_sums[2 * local_tokens :]], axis=0
    )
    received = with_halo(outward.astype(jnp.bfloat16), (("tok", 0),), local_tokens).astype(
        outward.dtype
    )
    token_sums = (
        partial_sums[local_tokens : 2 * local_tokens]
        + received[:local_tokens]
        + received[3 * local_tokens :]
    )
    stream = token_sums / atom_counts.astype(jnp.float32)[:, None]
    pair_bias = jnp.einsum(
        "ijc,ch->hij", pair_rep, pair_w, preferred_element_type=jnp.float32
    ).astype(jnp.bfloat16)
    head_size = C // H
    for layer_index in range(NB):
        normed = layer_norm(stream).astype(jnp.bfloat16)
        projected = jnp.dot(
            normed, tok_qkv_w[layer_index], preferred_element_type=jnp.float32
        ).astype(jnp.bfloat16)
        token_queries = projected[:, :C].reshape(local_tokens, H, head_size)
        token_keyvals = projected[:, C:]
        bias_layer = pair_bias[layer_index * H : (layer_index + 1) * H]

        def attend(running, shard_rows, offset, token_queries=token_queries, bias_layer=bias_layer):
            maximum, denominator, accumulated = running
            piece_rows = shard_rows.shape[0]
            key_heads = shard_rows[:, :C].reshape(piece_rows, H, head_size)
            value_heads = shard_rows[:, C:].reshape(piece_rows, H, head_size)
            scores = jnp.einsum(
                "qhd,khd->hqk", token_queries, key_heads, preferred_element_type=jnp.float32
            ) * head_size ** (-0.5)
            scores = scores + bias_layer.astype(jnp.float32)
            newmax = jnp.maximum(maximum, jnp.max(scores, axis=-1))
            powers = jnp.exp(scores - newmax[..., None])
            denominator = jnp.sum(powers, axis=-1)
            update = jnp.einsum(
                "hqk,khd->hqd",
                powers.astype(jnp.bfloat16),
                value_heads,
                preferred_element_type=jnp.float32,
            )
            accumulated = update
            return (newmax, denominator, accumulated)

        initial = (
            jnp.full((H, local_tokens), -1e30, jnp.float32),
            jnp.zeros((H, local_tokens), jnp.float32),
            jnp.zeros((H, local_tokens, head_size), jnp.float32),
        )
        maximum, denominator, accumulated = attend(
            initial, lax.all_gather(token_keyvals, "tok", axis=0, tiled=True), jnp.int32(0)
        )
        mixed_heads = (
            (accumulated / denominator[..., None])
            .transpose(1, 0, 2)
            .reshape(local_tokens, C)
            .astype(jnp.bfloat16)
        )
        stream = stream + jnp.dot(
            mixed_heads, tok_out_w[layer_index], preferred_element_type=jnp.float32
        )
    token_out = stream.astype(jnp.bfloat16)
    token_carry = jnp.dot(token_out, bcast_w, preferred_element_type=jnp.float32).astype(
        jnp.bfloat16
    )
    token_table = with_halo(token_carry, (("tok", 0),), local_tokens)
    picked = jnp.take(token_table, atom_token - first_token + local_tokens, axis=0)
    atom_out = (atom_hidden.astype(jnp.float32) + picked.astype(jnp.float32)).astype(jnp.bfloat16)
    return (atom_out, token_out)


def solution(mesh):
    placed = (
        P(("seed", "tok"), None),
        P("tok", None),
        P("tok"),
        P("tok"),
        P("tok", None, None),
        P(),
        P(),
        P(),
        P(),
        P(),
        P(),
        P(),
    )
    return jax.shard_map(
        local,
        mesh=mesh,
        in_specs=placed,
        out_specs=(P(("seed", "tok"), None), P(("seed", "tok"), None)),
        check_vma=False,
    )
```

profile of v0, /device:TPU:28, one launch (start us, length us, event | category | flops | bytes accessed | tf_op | source)
XLA Modules:
  0.0 91.4 jit_solution(15114924536646293480)
XLA Ops:
  0.6 0.0 copy-start
  0.6 1.1 %convert_reduce_fusion = f32[256]{0:T(256)S(1)} fusion(bf16[256,128]{1,0:T(8,128)(2,1)} %param.12), kind=kLoop, calls=%fused_computation.60 | loop fusion | flops 65280 | bytes 66560 | tf_op jit(solution)/shard_map/reduce_sum | solution.py:34
  1.8 1.0 %fusion.56 = f32[256]{0:T(256)S(1)} fusion(bf16[256,128]{1,0:T(8,128)(2,1)} %param.12, f32[256]{0:T(256)S(1)} %broadcast_multiply_fusion), kind=kLoop, calls=%fused_computation.64 | loop fusion | flops 130816 | bytes 67584 | tf_op jit(solution)/shard_map/reduce_sum | solution.py:36
  2.8 1.2 %convolution_convert_fusion = bf16[256,384]{1,0:T(8,128)(2,1)S(1)} fusion(bf16[128,384]{1,0:T(8,128)(2,1)} %param.17, bf16[256,128]{1,0:T(8,128)(2,1)} %param.12, f32[256]{0:T(256)S(1)} %add_rsqrt_fusion, f32[256]{0:T(256)S(1)} %broadcast_multiply_fusion), kind=kOutput, calls=%fused_computation.28 | convolution fusion | flops 25395200 | bytes 362496 | tf_op jit(solution)/shard_map/dot_general | solution.py:99
  4.0 1.9 %collective-permute-start = (bf16[48,256]{1,0:T(8,128)(2,1)S(1)}, bf16[48,256]{1,0:T(8,128)(2,1)S(1)}, u32[]{:S(2)}, u32[]{:S(2)}) collective-permute-start(bf16[48,256]{1,0:T(8,128)(2,1)S(1)} %get-tuple-element.12), channel_id=1, source_target_pairs={{0,1},{1,2},{2,3},{3,4},{4,5},{5,6},{6,7},{8,9},{9,10},{10,11},{11... | collective-permute-start | bytes 73736 | tf_op jit(solution)/shard_map/ppermute | solution.py:24
  5.9 4.5 %collective-permute-start.1 = (bf16[48,256]{1,0:T(8,128)(2,1)S(1)}, bf16[48,256]{1,0:T(8,128)(2,1)S(1)}, u32[]{:S(2)}, u32[]{:S(2)}) collective-permute-start(bf16[48,256]{1,0:T(8,128)(2,1)S(1)} %get-tuple-element.13), channel_id=1, source_target_pairs={{1,0},{2,1},{3,2},{4,3},{5,4},{6,5},{7,6},{9,8},{10,9},{11,10},{12... | collective-permute-start | bytes 73736 | tf_op jit(solution)/shard_map/ppermute | solution.py:26
  10.5 0.1 fusion.81
  10.6 0.1 fusion.78
  10.7 1.5 %fusion.75 = bf16[32,32,256]{2,0,1:T(8,128)(2,1)S(1)} fusion(bf16[32,256,128]{2,1,0:T(8,128)(2,1)S(1)} %copy-done, bf16[128,32]{0,1:T(8,128)(2,1)} %param.22), kind=kOutput, calls=%fused_computation.93 | convolution fusion | flops 67108864 | bytes 2629632 | tf_op jit(solution)/shard_map/ijc,ch->hij/dot_general | solution.py:130
  12.2 0.2 reshape.167
  12.4 1.9 %reshape.175 = f32[8,32,4,128]{3,2,1,0:T(4,128)} reshape(bf16[256,512]{1,0:T(8,128)(2,1)} %param.13) | data formatting | bytes 786432 | tf_op jit(solution)/shard_map/convert_element_type | solution.py:49
  14.3 5.0 %gather_fusion = bf16[1024,256]{1,0:T(8,128)(2,1)} fusion(bf16[352,256]{1,0:T(8,128)(2,1)S(1)} %pad_maximum_fusion, s32[1024]{0:T(1024)S(1)} %fusion.78), kind=kCustom, calls=%fused_computation | custom fusion | bytes 1052672 | tf_op jit(solution)/shard_map/gather | solution.py:107
  19.3 1.9 %fusion.86 = (bf16[8,128,128]{2,1,0:T(8,128)(2,1)}, bf16[8,128,128]{2,1,0:T(8,128)(2,1)}) fusion(bf16[8,128,256]{2,1,0:T(8,128)(2,1)} %bitcast.81), kind=kLoop, calls=%fused_computation.118 | loop fusion | bytes 1048576 | tf_op jit(solution)/shard_map/slice | solution.py:44
  21.2 1.8 %copy.39 = bf16[8,128,128]{1,2,0:T(8,128)(2,1)} copy(bf16[8,128,128]{2,1,0:T(8,128)(2,1)} %get-tuple-element.10) | data formatting | bytes 524288
  23.0 1.8 %copy.38 = bf16[8,128,128]{1,2,0:T(8,128)(2,1)} copy(bf16[8,128,128]{2,1,0:T(8,128)(2,1)} %get-tuple-element.11) | data formatting | bytes 524288
  24.8 1.3 %fusion.89 = (f32[8,4,32]{2,1,0:T(4,128)S(1)}, f32[8,4,32,128]{3,2,1,0:T(8,128)S(1)}) fusion(f32[8,32,4,128]{3,2,1,0:T(4,128)S(1)} %copy-done.1, bf16[8,128,4,32]{1,3,2,0:T(8,128)(2,1)} %bitcast.84, bf16[8,32,4,32]{3,2,1,0:T(4,128)(2,1)S(1)} %reshape.167, pred[8,128]{1,0:T(8,128)(4,1)S(1)} %fusion.81), kind=kOutput, calls=%fused_computation.121 | convolution fusion | flops 8911872 | bytes 1381376 | tf_op jit(solution)/shard_map/wqhd,wkhd->whqk/dot_general | solution.py:46
  26.2 0.4 fusion.38
  26.6 1.3 %fusion.17 = bf16[8,32,4,32]{1,3,2,0:T(8,128)(2,1)S(1)} fusion(bf16[8,128,4,32]{1,3,2,0:T(8,128)(2,1)} %bitcast.87, f32[8,4,32,128]{3,2,1,0:T(8,128)S(1)} %get-tuple-element.17, f32[8,32,4]{1,2,0:T(4,128)S(1)} %bitcast.88, f32[8,4,32]{2,1,0:T(4,128)S(1)} %get-tuple-element.16), kind=kOutput, calls=%fused_computation.20 | convolution fusion | flops 8716288 | bytes 860160 | tf_op jit(solution)/shard_map/whqk,wkhd->wqhd/dot_general | solution.py:64
  27.9 0.2 copy.28
  28.1 0.2 convert_element_type.109
  28.3 0.2 fusion.28
  28.5 0.6 copy-done.7
  29.1 0.2 convolution_maximum_fusion
  29.4 0.2 fusion.52
  29.6 0.2 fusion.90
  29.9 1.9 %collective-permute-start.2 = (bf16[32,768]{1,0:T(8,128)(2,1)S(1)}, bf16[32,768]{1,0:T(8,128)(2,1)S(1)}, u32[]{:S(2)}, u32[]{:S(2)}) collective-permute-start(bf16[32,768]{1,0:T(8,128)(2,1)S(1)} %get-tuple-element.14), channel_id=1, source_target_pairs={{0,1},{1,2},{2,3},{3,4},{4,5},{5,6},{6,7},{8,9},{9,10},{10,11},{11... | collective-permute-start | bytes 147464 | tf_op jit(solution)/shard_map/ppermute | solution.py:24
  31.8 4.5 %collective-permute-start.3 = (bf16[32,768]{1,0:T(8,128)(2,1)S(1)}, bf16[32,768]{1,0:T(8,128)(2,1)S(1)}, u32[]{:S(2)}, u32[]{:S(2)}) collective-permute-start(bf16[32,768]{1,0:T(8,128)(2,1)S(1)} %get-tuple-element.15), channel_id=1, source_target_pairs={{1,0},{2,1},{3,2},{4,3},{5,4},{6,5},{7,6},{9,8},{10,9},{11,10},{12... | collective-permute-start | bytes 147464 | tf_op jit(solution)/shard_map/ppermute | solution.py:26
  36.4 0.3 copy.48
  36.7 1.4 %collective-permute-done.3 = bf16[32,768]{1,0:T(8,128)(2,1)S(1)} collective-permute-done((bf16[32,768]{1,0:T(8,128)(2,1)S(1)}, bf16[32,768]{1,0:T(8,128)(2,1)S(1)}, u32[]{:S(2)}, u32[]{:S(2)}) %collective-permute-start.3) | collective-permute-done | bytes 49184 | tf_op jit(solution)/shard_map/ppermute | solution.py:26
  38.1 0.2 fusion.82
  38.3 0.2 multiply_reduce_fusion.1
  38.5 0.4 copy-done.3
  38.9 2.8 %fusion.6 = bf16[32,2304]{1,0:T(8,128)(2,1)S(1)} fusion(bf16[2,768,2304]{2,1,0:T(8,128)(2,1)} %param.20, f32[32,768]{1,0:T(8,128)S(1)} %get-tuple-element.5, f32[32]{0:T(128)S(1)} %add_rsqrt_fusion.2, f32[32]{0:T(128)S(1)} %broadcast_multiply_fusion.2), kind=kOutput, calls=%fused_computation.8 | convolution fusion | flops 113393664 | bytes 3784960 | tf_op jit(solution)/shard_map/dot_general | solution.py:136
  41.8 0.8 reshape.169
  42.6 10.4 %all_gather.6 = bf16[256,1536]{1,0:T(8,128)(2,1)S(1)} all-gather(bf16[32,1536]{1,0:T(8,128)(2,1)S(1)} %slice.120), channel_id=1, replica_groups=mesh['seed'=4,'tok'=8] {'tok'}, dimensions={0}, use_global_device_ids=true | all-gather | bytes 884736 | tf_op jit(solution)/shard_map/all_gather | solution.py:170
  53.0 0.1 fusion.85
  53.1 0.9 copy.29
  54.0 1.4 %fusion.91 = (f32[16,32]{1,0:T(8,128)S(1)}, f32[16,32,256]{2,1,0:T(8,128)S(1)}) fusion(bf16[32,32,256]{2,1,0:T(8,128)(2,1)S(1)} %copy.48, bf16[256,16,48]{0,2,1:T(8,128)(2,1)} %bitcast.83, bf16[32,16,48]{2,1,0:T(8,128)(2,1)} %reshape.169), kind=kOutput, calls=%fused_computation.123 | convolution fusion | flops 13106688 | bytes 1230848 | tf_op jit(solution)/shard_map/qhd,khd->hqk/dot_general | solution.py:148
  55.4 0.9 copy.32
  56.3 0.3 fusion.40
  56.5 1.3 %fusion.26 = bf16[32,16,48]{2,0,1:T(8,128)(2,1)S(1)} fusion(bf16[256,16,48]{0,2,1:T(8,128)(2,1)} %bitcast.85, f32[16,32,256]{2,1,0:T(8,128)S(1)} %get-tuple-element.21, f32[16,32]{1,0:T(8,128)S(1)} %broadcast_maximum_fusion.1, f32[32,16]{0,1:T(8,128)S(1)} %bitcast.89), kind=kOutput, calls=%fused_computation.33 | convolution fusion | flops 12894208 | bytes 970752 | tf_op jit(solution)/shard_map/hqk,khd->hqd/dot_general | solution.py:155
  57.8 0.1 copy.33
  57.9 0.2 convert_element_type.123
  58.1 1.7 %fusion.92 = (f32[32]{0:T(128)S(1)}, f32[32,768]{1,0:T(8,128)S(1)}) fusion(f32[32,768]{1,0:T(8,128)S(1)} %copy-done.4, bf16[32,768]{1,0:T(8,128)(2,1)S(1)} %convert_element_type.123, bf16[2,768,768]{2,1,0:T(8,128)(2,1)} %param.21), kind=kOutput, calls=%fused_computation.124 | convolution fusion | flops 37797856 | bytes 1425536 | tf_op jit(solution)/shard_map/dot_general | solution.py:178
  59.8 0.2 multiply_reduce_fusion
  60.0 2.8 %fusion.9 = bf16[32,2304]{1,0:T(8,128)(2,1)S(1)} fusion(bf16[2,768,2304]{2,1,0:T(8,128)(2,1)} %param.20, f32[32,768]{1,0:T(8,128)S(1)} %get-tuple-element.23, f32[32]{0:T(128)S(1)} %add_rsqrt_fusion.1, f32[32]{0:T(128)S(1)} %broadcast_multiply_fusion.1), kind=kOutput, calls=%fused_computation.9 | convolution fusion | flops 113393664 | bytes 3784960 | tf_op jit(solution)/shard_map/dot_general | solution.py:136
  62.8 0.8 reshape.172
  63.6 10.2 %all_gather.7 = bf16[256,1536]{1,0:T(8,128)(2,1)S(1)} all-gather(bf16[32,1536]{1,0:T(8,128)(2,1)S(1)} %slice.125), channel_id=1, replica_groups=mesh['seed'=4,'tok'=8] {'tok'}, dimensions={0}, use_global_device_ids=true | all-gather | bytes 884736 | tf_op jit(solution)/shard_map/all_gather | solution.py:170
  73.8 0.1 fusion.84
  73.9 0.9 copy.34
  74.8 1.4 %fusion.93 = (f32[16,32]{1,0:T(8,128)S(1)}, f32[16,32,256]{2,1,0:T(8,128)S(1)}) fusion(bf16[32,32,256]{2,1,0:T(8,128)(2,1)S(1)} %copy.48, bf16[256,16,48]{0,2,1:T(8,128)(2,1)} %bitcast.82, bf16[32,16,48]{2,1,0:T(8,128)(2,1)} %reshape.172), kind=kOutput, calls=%fused_computation.125 | convolution fusion | flops 13106688 | bytes 1230848 | tf_op jit(solution)/shard_map/qhd,khd->hqk/dot_general | solution.py:148
  76.1 0.9 copy.36
  77.1 0.3 fusion.42
  77.3 1.3 %fusion.27 = bf16[32,16,48]{2,0,1:T(8,128)(2,1)S(1)} fusion(bf16[256,16,48]{0,2,1:T(8,128)(2,1)} %bitcast.86, f32[16,32,256]{2,1,0:T(8,128)S(1)} %get-tuple-element.25, f32[16,32]{1,0:T(8,128)S(1)} %broadcast_maximum_fusion, f32[32,16]{0,1:T(8,128)S(1)} %bitcast.90), kind=kOutput, calls=%fused_computation.34 | convolution fusion | flops 12894208 | bytes 970752 | tf_op jit(solution)/shard_map/hqk,khd->hqd/dot_general | solution.py:155
  78.6 0.1 copy.37
  78.7 0.2 convert_element_type.129
  78.9 1.6 %fusion.35 = bf16[32,768]{1,0:T(8,128)(2,1)S(1)} fusion(f32[32,768]{1,0:T(8,128)S(1)} %copy-done.6, bf16[32,768]{1,0:T(8,128)(2,1)S(1)} %convert_element_type.129, bf16[2,768,768]{2,1,0:T(8,128)(2,1)} %param.21), kind=kOutput, calls=%fused_computation.39 | convolution fusion | flops 37797888 | bytes 1376256 | tf_op jit(solution)/shard_map/dot_general | solution.py:178
  80.5 0.0 copy-start.9
  80.5 0.1 convolution_convert_fusion.1
  80.6 3.3 %collective-permute-start.5 = (bf16[32,128]{1,0:T(8,128)(2,1)S(1)}, bf16[32,128]{1,0:T(8,128)(2,1)S(1)}, u32[]{:S(2)}, u32[]{:S(2)}) collective-permute-start(bf16[32,128]{1,0:T(8,128)(2,1)S(1)} %convolution_convert_fusion.1), channel_id=1, source_target_pairs={{1,0},{2,1},{3,2},{4,3},{5,4},{6,5},{7,6},{9,8},{10,9},{11,10},{12... | collective-permute-start | bytes 24584 | tf_op jit(solution)/shard_map/ppermute | solution.py:26
  84.0 1.9 %collective-permute-start.4 = (bf16[32,128]{1,0:T(8,128)(2,1)S(1)}, bf16[32,128]{1,0:T(8,128)(2,1)S(1)}, u32[]{:S(2)}, u32[]{:S(2)}) collective-permute-start(bf16[32,128]{1,0:T(8,128)(2,1)S(1)} %convolution_convert_fusion.1), channel_id=1, source_target_pairs={{0,1},{1,2},{2,3},{3,4},{4,5},{5,6},{6,7},{8,9},{9,10},{10,11},{11... | collective-permute-start | bytes 24584 | tf_op jit(solution)/shard_map/ppermute | solution.py:24
  85.9 3.9 %collective-permute-done.4 = bf16[32,128]{1,0:T(8,128)(2,1)S(1)} collective-permute-done((bf16[32,128]{1,0:T(8,128)(2,1)S(1)}, bf16[32,128]{1,0:T(8,128)(2,1)S(1)}, u32[]{:S(2)}, u32[]{:S(2)}) %collective-permute-start.4) | collective-permute-done | bytes 8224 | tf_op jit(solution)/shard_map/ppermute | solution.py:24
  89.9 0.9 gather_fusion.1
  90.7 0.7 add_convert_fusion
  (54 shorter events, 0.2 us)
Async XLA Ops:
  0.6 10.0 %copy-start = (bf16[32,256,128]{2,1,0:T(8,128)(2,1)S(1)}, bf16[32,256,128]{2,1,0:T(8,128)(2,1)}, u32[]{:S(2)}) copy-start(bf16[32,256,128]{2,1,0:T(8,128)(2,1)} %param.16) | copy-start | bytes 6291460
  4.0 10.3 %collective-permute-start = (bf16[48,256]{1,0:T(8,128)(2,1)S(1)}, bf16[48,256]{1,0:T(8,128)(2,1)S(1)}, u32[]{:S(2)}, u32[]{:S(2)}) collective-permute-start(bf16[48,256]{1,0:T(8,128)(2,1)S(1)} %get-tuple-element.12), channel_id=1, source_target_pairs={{0,1},{1,2},{2,3},{3,4},{4,5},{5,6},{6,7},{8,9},{9,10},{10,11},{11... | collective-permute-start | bytes 73736 | tf_op jit(solution)/shard_map/ppermute | solution.py:24
  5.9 8.4 %collective-permute-start.1 = (bf16[48,256]{1,0:T(8,128)(2,1)S(1)}, bf16[48,256]{1,0:T(8,128)(2,1)S(1)}, u32[]{:S(2)}, u32[]{:S(2)}) collective-permute-start(bf16[48,256]{1,0:T(8,128)(2,1)S(1)} %get-tuple-element.13), channel_id=1, source_target_pairs={{1,0},{2,1},{3,2},{4,3},{5,4},{6,5},{7,6},{9,8},{10,9},{11,10},{12... | collective-permute-start | bytes 73736 | tf_op jit(solution)/shard_map/ppermute | solution.py:26
  19.3 5.5 %copy-start.1 = (f32[8,32,4,128]{3,2,1,0:T(4,128)S(1)}, f32[8,32,4,128]{3,2,1,0:T(4,128)}, u32[]{:S(2)}) copy-start(f32[8,32,4,128]{3,2,1,0:T(4,128)} %reshape.175) | copy-start | bytes 1572868
  24.8 3.5 %copy-start.2 = (bf16[256,128]{1,0:T(8,128)(2,1)S(1)}, bf16[256,128]{1,0:T(8,128)(2,1)}, u32[]{:S(2)}) copy-start(bf16[256,128]{1,0:T(8,128)(2,1)} %param.12) | copy-start | bytes 196612
  24.8 3.5 %copy-start.12 = (bf16[128,128]{1,0:T(8,128)(2,1)S(1)}, bf16[128,128]{1,0:T(8,128)(2,1)}, u32[]{:S(2)}) copy-start(bf16[128,128]{1,0:T(8,128)(2,1)} %param.18) | copy-start | bytes 98308
  26.2 3.0 %copy-start.10 = (bf16[128,768]{1,0:T(8,128)(2,1)S(1)}, bf16[128,768]{1,0:T(8,128)(2,1)}, u32[]{:S(2)}) copy-start(bf16[128,768]{1,0:T(8,128)(2,1)} %param.19) | copy-start | bytes 589828
  26.6 2.8 %copy-start.13 = (s32[256]{0:T(256)S(1)}, s32[256]{0:T(256)}, u32[]{:S(2)}) copy-start(s32[256]{0:T(256)} %param.14) | copy-start | bytes 3076
  27.9 8.5 %copy-start.14 = (s32[32]{0:T(128)S(1)}, s32[32]{0:T(128)}, u32[]{:S(2)}) copy-start(s32[32]{0:T(128)} %param.15) | copy-start | bytes 388
  28.5 0.6 copy-start.7
  29.9 6.8 %collective-permute-start.2 = (bf16[32,768]{1,0:T(8,128)(2,1)S(1)}, bf16[32,768]{1,0:T(8,128)(2,1)S(1)}, u32[]{:S(2)}, u32[]{:S(2)}) collective-permute-start(bf16[32,768]{1,0:T(8,128)(2,1)S(1)} %get-tuple-element.14), channel_id=1, source_target_pairs={{0,1},{1,2},{2,3},{3,4},{4,5},{5,6},{6,7},{8,9},{9,10},{10,11},{11... | collective-permute-start | bytes 147464 | tf_op jit(solution)/shard_map/ppermute | solution.py:24
  31.8 6.3 %collective-permute-start.3 = (bf16[32,768]{1,0:T(8,128)(2,1)S(1)}, bf16[32,768]{1,0:T(8,128)(2,1)S(1)}, u32[]{:S(2)}, u32[]{:S(2)}) collective-permute-start(bf16[32,768]{1,0:T(8,128)(2,1)S(1)} %get-tuple-element.15), channel_id=1, source_target_pairs={{1,0},{2,1},{3,2},{4,3},{5,4},{6,5},{7,6},{9,8},{10,9},{11,10},{12... | collective-permute-start | bytes 147464 | tf_op jit(solution)/shard_map/ppermute | solution.py:26
  38.3 0.6 copy-start.3
  56.3 1.8 %copy-start.4 = (f32[32,768]{1,0:T(8,128)S(1)}, f32[32,768]{1,0:T(8,128)}, u32[]{:S(2)}) copy-start(f32[32,768]{1,0:T(8,128)} %copy-done.3) | copy-start | bytes 294916
  59.8 3.9 %copy-start.5 = (f32[32,768]{1,0:T(8,128)}, f32[32,768]{1,0:T(8,128)S(1)}, u32[]{:S(2)}) copy-start(f32[32,768]{1,0:T(8,128)S(1)} %get-tuple-element.23) | copy-start | bytes 294916
  76.1 2.7 %copy-start.6 = (f32[32,768]{1,0:T(8,128)S(1)}, f32[32,768]{1,0:T(8,128)}, u32[]{:S(2)}) copy-start(f32[32,768]{1,0:T(8,128)} %copy-done.5) | copy-start | bytes 294916
  77.1 3.4 %copy-start.11 = (bf16[768,128]{1,0:T(8,128)(2,1)S(1)}, bf16[768,128]{1,0:T(8,128)(2,1)}, u32[]{:S(2)}) copy-start(bf16[768,128]{1,0:T(8,128)(2,1)} %param.23) | copy-start | bytes 589828
  77.1 13.7 %copy-start.8 = (bf16[256,128]{1,0:T(8,128)(2,1)S(1)}, bf16[256,128]{1,0:T(8,128)(2,1)}, u32[]{:S(2)}) copy-start(bf16[256,128]{1,0:T(8,128)(2,1)} %copy-done.7) | copy-start | bytes 196612
  80.5 11.0 %copy-start.9 = (bf16[32,768]{1,0:T(8,128)(2,1)}, bf16[32,768]{1,0:T(8,128)(2,1)S(1)}, u32[]{:S(2)}) copy-start(bf16[32,768]{1,0:T(8,128)(2,1)S(1)} %fusion.35) | copy-start | bytes 147460
  80.6 5.3 %collective-permute-start.5 = (bf16[32,128]{1,0:T(8,128)(2,1)S(1)}, bf16[32,128]{1,0:T(8,128)(2,1)S(1)}, u32[]{:S(2)}, u32[]{:S(2)}) collective-permute-start(bf16[32,128]{1,0:T(8,128)(2,1)S(1)} %convolution_convert_fusion.1), channel_id=1, source_target_pairs={{1,0},{2,1},{3,2},{4,3},{5,4},{6,5},{7,6},{9,8},{10,9},{11,10},{12... | collective-permute-start | bytes 24584 | tf_op jit(solution)/shard_map/ppermute | solution.py:26
  84.0 5.9 %collective-permute-start.4 = (bf16[32,128]{1,0:T(8,128)(2,1)S(1)}, bf16[32,128]{1,0:T(8,128)(2,1)S(1)}, u32[]{:S(2)}, u32[]{:S(2)}) collective-permute-start(bf16[32,128]{1,0:T(8,128)(2,1)S(1)} %convolution_convert_fusion.1), channel_id=1, source_target_pairs={{0,1},{1,2},{2,3},{3,4},{4,5},{5,6},{6,7},{8,9},{9,10},{10,11},{11... | collective-permute-start | bytes 24584 | tf_op jit(solution)/shard_map/ppermute | solution.py:24
where the time goes:
time: 92.2 us; the launch traced here: 91.4 us
  local copies, waits for them, and re-layouts  21.1 us (23%)
  matrix products  20.6 us (22%)
  blocking collectives  20.6 us (22%)
  starting transfers between devices  18.2 us (20%)
  waiting for transfers between devices  5.31 us (6%)
  other arithmetic  4.58 us (5%)
  between operations  1.11 us (1%)
    all_gather x2, blocking collectives, local(): lax.all_gather(token_keyvals, 'tok', axis=0, tiled=True)  20.6 us
    ppermute x3, starting transfers between devices, with_halo(): lax.ppermute(head, axis, [((i + 1) % count, i) for i in range(ends)])  12.4 us
    ppermute x3, starting transfers between devices, with_halo(): lax.ppermute(tail, axis, [(i, (i + 1) % count) for i in range(ends)])  5.76 us
    dot_general x2, matrix products, local(): jnp.dot(normed, tok_qkv_w[layer_index], preferred_element_type=jnp.float32)  5.56 us
    gather x1, local copies, waits for them, and re-layouts, local(): keyvals = padded[gather_index]  4.96 us
    unnamed x32, local copies, waits for them, and re-layouts  4.71 us
    ppermute x3, waiting for transfers between devices, with_halo(): lax.ppermute(tail, axis, [(i, (i + 1) % count) for i in range(ends)])  3.92 us
    dot_general x2, matrix products, local(): jnp.dot(mixed_heads, tok_out_w[layer_index], preferred_element_type=jnp.f...  3.3 us
  transfers between devices with their start and end apart: 6, of which 2 were waited for; matrix products, arithmetic and copies ran while one was open for 4% of the time, Pallas kernels for 0%

commit v1 on v0

v1 whole, which is shorter than its diff:
```python
import functools

import jax
import jax.numpy as jnp
from jax import lax
from jax.experimental import pallas as pl
from jax.experimental.pallas import tpu as pltpu
from jax.sharding import PartitionSpec as P

H = 16
AH = 4
QW = 32
KW = 128
HALO = 48
SIDE = QW + HALO
EXTRA = 16
F32 = jnp.float32
BF16 = jnp.bfloat16


def layer_norm(values):
    average = jnp.mean(values, axis=-1, keepdims=True)
    centred = values - average
    variance = jnp.mean(centred * centred, axis=-1, keepdims=True)
    return centred * lax.rsqrt(variance + 1e-05)


def dot(a, b):
    return jnp.dot(a, b, preferred_element_type=F32)


def dot_nt(a, b):
    return lax.dot_general(a, b, (((1,), (1,)), ((), ())), preferred_element_type=F32)


def dot_tn(a, b):
    return lax.dot_general(a, b, (((0,), (0,)), ((), ())), preferred_element_type=F32)


def wanted_tokens(tokens, count):
    first = lax.axis_index("tok") * tokens
    row = lax.broadcasted_iota(jnp.int32, (count, 1), 0)
    sides = jnp.where(row == tokens, first - 1, jnp.where(row == tokens + 1, first + tokens, -9))
    return jnp.where(row < tokens, first + row, sides)


def kernel(
    n,
    single_hbm,
    bias_hbm,
    token_hbm,
    pair_hbm,
    qkv_hbm,
    aout_hbm,
    agg_hbm,
    tqkv_hbm,
    tout_hbm,
    pairw_hbm,
    hidden_out,
    final_out,
    xs,
    bs,
    tok_mid,
    tok_low,
    tok_high,
    pair,
    qkv_w,
    aout_w,
    agg_w,
    tqkv_w,
    tout_w,
    pair_w,
    proj,
    mixed,
    gathered,
    pbias,
    local_sem,
    halo_send,
    halo_recv,
    gather_send,
    gather_recv,
):
    atoms, ca = single_hbm.shape
    tokens = pair_hbm.shape[0]
    blocks, c, _ = tout_hbm.shape
    all_tokens = n * tokens
    ext_atoms = atoms + 2 * QW
    ext_tokens = tokens + EXTRA
    used = tokens + 2
    me = lax.axis_index("tok")
    right = lax.rem(me + 1, n)
    left = lax.rem(me + n - 1, n)

    barrier = pltpu.get_barrier_semaphore()
    for k in range(1, n):
        pl.semaphore_signal(
            barrier,
            inc=1,
            device_id={"tok": lax.rem(me + k, n)},
            device_id_type=pl.DeviceIdType.MESH,
        )

    moves = [
        (single_hbm, xs.at[SIDE : SIDE + atoms]),
        (bias_hbm, bs.at[QW : QW + atoms]),
        (token_hbm, tok_mid),
        (qkv_hbm, qkv_w),
        (aout_hbm, aout_w),
        (agg_hbm, agg_w),
        (pairw_hbm, pair_w),
        (pair_hbm, pair.at[0:tokens]),
        (tqkv_hbm.at[0], tqkv_w.at[0]),
        (tout_hbm.at[0], tout_w.at[0]),
        (tqkv_hbm.at[1], tqkv_w.at[1]),
        (tout_hbm.at[1], tout_w.at[1]),
    ]
    copies = [
        pltpu.make_async_copy(src, dst, local_sem.at[i]) for i, (src, dst) in enumerate(moves)
    ]
    for copy in copies[:8]:
        copy.start()
    (c_single, c_bias, c_token, c_qkv, c_aout, c_agg, c_pairw, c_pair) = copies[:8]
    c_tqkv = [copies[8], copies[10]]
    c_tout = [copies[9], copies[11]]

    pl.semaphore_wait(barrier, n - 1)
    halo_moves = [
        (single_hbm.at[atoms - SIDE : atoms], xs.at[0:SIDE], right),
        (single_hbm.at[0:SIDE], xs.at[SIDE + atoms : 2 * SIDE + atoms], left),
        (bias_hbm.at[atoms - QW : atoms], bs.at[0:QW], right),
        (bias_hbm.at[0:QW], bs.at[QW + atoms : 2 * QW + atoms], left),
        (token_hbm, tok_low, right),
        (token_hbm, tok_high, left),
        (pair_hbm.at[tokens - 1], pair.at[tokens], right),
        (pair_hbm.at[0], pair.at[tokens + 1], left),
    ]
    halos = [
        pltpu.make_async_remote_copy(
            src_ref=src,
            dst_ref=dst,
            send_sem=halo_send.at[i],
            recv_sem=halo_recv.at[i],
            device_id={"tok": to},
            device_id_type=pl.DeviceIdType.MESH,
        )
        for i, (src, dst, to) in enumerate(halo_moves)
    ]
    for copy in halos:
        copy.start()
    for copy in copies[8:]:
        copy.start()

    def pair_rows(t):
        rows = dot_nt(pair_w[...], pair[t]).astype(BF16)
        for b in range(blocks):
            pbias[b, t * H : (t + 1) * H, :] = rows[b * H : (b + 1) * H]

    c_single.wait()
    c_bias.wait()
    c_token.wait()
    c_qkv.wait()
    width = ca // AH
    lane = lax.broadcasted_iota(jnp.int32, (QW, ca), 1)
    head_masks = [(lane // width == h).astype(F32) for h in range(AH)]
    head_picks = [m.astype(BF16) for m in head_masks]
    key_lane = lax.broadcasted_iota(jnp.int32, (1, KW), 1)

    def project(rows):
        return dot(layer_norm(rows.astype(F32)).astype(BF16), qkv_w[...]).astype(BF16)

    def window(w):
        q = proj[HALO + QW * w : HALO + QW * (w + 1), :ca]
        keys = proj[QW * w : QW * w + KW, ca : 2 * ca]
        values = proj[QW * w : QW * w + KW, 2 * ca :]
        spread = jnp.concatenate([q * pick for pick in head_picks], axis=0)
        bias = jnp.concatenate(
            [bs[QW * w : QW * (w + 1), h * KW : (h + 1) * KW] for h in range(AH)], axis=0
        )
        scores = dot_nt(spread, keys) * width ** (-0.5) + bias.astype(F32)
        position = me * atoms - SIDE + QW * w + key_lane
        inside = (position >= 0) & (position < n * atoms)
        scores = jnp.where(inside, scores, -1000000000.0)
        powers = jnp.exp(scores - jnp.max(scores, axis=-1, keepdims=True))
        total = jnp.sum(powers, axis=-1, keepdims=True)
        heads = dot(powers.astype(BF16), values) / total
        out = heads[:QW] * head_masks[0]
        for h in range(1, AH):
            out = out + heads[h * QW : (h + 1) * QW] * head_masks[h]
        mixed[QW * w : QW * (w + 1), :] = out.astype(BF16)

    windows = range(ext_atoms // QW)
    inner = [w for w in windows if QW * w >= SIDE and QW * w + KW <= SIDE + atoms]
    proj[SIDE : SIDE + atoms, :] = project(xs[SIDE : SIDE + atoms])
    for w in inner:
        window(w)
    for copy in halos[:6]:
        copy.wait()
    edges = project(jnp.concatenate([xs[:SIDE], xs[SIDE + atoms :]], axis=0))
    proj[:SIDE, :] = edges[:SIDE]
    proj[SIDE + atoms :, :] = edges[SIDE:]
    for w in windows:
        if w not in inner:
            window(w)
    c_aout.wait()
    c_agg.wait()
    own_rows = xs[HALO : HALO + ext_atoms].astype(F32)
    hidden = (own_rows + dot(mixed[...], aout_w[...])).astype(BF16)
    hidden_out[...] = hidden[QW : QW + atoms]
    lifted = jnp.maximum(dot(hidden, agg_w[...]), 0.0)

    wanted = wanted_tokens(tokens, ext_tokens)
    near = jnp.concatenate(
        [tok_low[:, atoms - QW :], tok_mid[...], tok_high[:, :QW]], axis=1
    )
    member = (near == wanted).astype(F32)
    count = jnp.maximum(jnp.sum(member, axis=-1, keepdims=True), 1.0)
    picker = member.astype(BF16)
    upper = lifted.astype(BF16)
    lower = (lifted - upper.astype(F32)).astype(BF16)
    stream = (dot(picker, upper) + dot(picker, lower)) / count

    rows = used * H
    head_size = c // H
    row_token = lax.broadcasted_iota(jnp.int32, (rows, ext_tokens), 0) // H
    spreader = (row_token == lax.broadcasted_iota(jnp.int32, (rows, ext_tokens), 1)).astype(
        F32
    ).astype(BF16)
    col_token = lax.broadcasted_iota(jnp.int32, (ext_tokens, rows), 1) // H
    collector = (col_token == lax.broadcasted_iota(jnp.int32, (ext_tokens, rows), 0)).astype(
        F32
    ).astype(BF16)
    head_row = lax.broadcasted_iota(jnp.int32, (H, c), 0)
    head_lane = lax.broadcasted_iota(jnp.int32, (H, c), 1) // head_size
    tok_mask = (head_row == head_lane).astype(F32).astype(BF16)
    tok_mask = jnp.concatenate([tok_mask] * used, axis=0)
    own = pl.ds(pl.multiple_of(me * tokens, tokens), tokens)
    for b in range(blocks):
        normed = layer_norm(stream).astype(BF16)
        gathered[b, own, :] = normed[:tokens]
        sends = [
            pltpu.make_async_remote_copy(
                src_ref=gathered.at[b, own],
                dst_ref=gathered.at[b, own],
                send_sem=gather_send.at[b, k - 1],
                recv_sem=gather_recv.at[b, k - 1],
                device_id={"tok": lax.rem(me + k, n)},
                device_id_type=pl.DeviceIdType.MESH,
            )
            for k in range(1, n)
        ]
        for copy in sends:
            copy.start()
        if b == 0:
            c_pairw.wait()
            c_pair.wait()
            for copy in halos[6:]:
                copy.wait()
            for t in range(used):
                pair_rows(t)
        c_tqkv[b].wait()
        q = dot(normed, tqkv_w[b, :, :c]).astype(BF16)
        spread = dot(spreader, q).astype(BF16) * tok_mask
        c_tout[b].wait()
        for copy in sends:
            copy.wait()
        everyone = gathered[b]
        keys = dot(everyone, tqkv_w[b, :, c : 2 * c]).astype(BF16)
        scores = dot_nt(spread, keys) * head_size ** (-0.5) + pbias[b].astype(F32)
        powers = jnp.exp(scores - jnp.max(scores, axis=-1, keepdims=True))
        total = jnp.sum(powers, axis=-1, keepdims=True)
        values = dot(everyone, tqkv_w[b, :, 2 * c :]).astype(BF16)
        heads = (dot(powers.astype(BF16), values) / total).astype(BF16) * tok_mask
        mixed = dot(collector, heads).astype(BF16)
        stream = stream + dot(mixed, tout_w[b])

    final_out[...] = stream.astype(BF16)


def hand_over(final, hidden, token, bcast, atom_out, token_out):
    tokens = token_out.shape[0]
    token_out[...] = final[:tokens, :]
    carry = dot(final[...], bcast[...]).astype(BF16)
    mine = (token[...] == wanted_tokens(tokens, final.shape[0])).astype(F32).astype(BF16)
    atom_out[...] = (hidden[...].astype(F32) + dot_tn(mine, carry)).astype(BF16)


def local(
    atom_single,
    atom_bias,
    atom_token,
    atom_counts,
    pair_rep,
    atom_qkv_w,
    atom_out_w,
    agg_w,
    tok_qkv_w,
    tok_out_w,
    pair_w,
    bcast_w,
):
    n = lax.axis_size("tok")
    atoms, ca = atom_single.shape
    tokens, all_tokens, cz = pair_rep.shape
    blocks, c, _ = tok_out_w.shape
    operands = (
        atom_single,
        atom_bias,
        atom_token.reshape(1, atoms),
        pair_rep,
        atom_qkv_w,
        atom_out_w,
        agg_w,
        tok_qkv_w,
        tok_out_w,
        pair_w.T,
    )
    dma = pltpu.SemaphoreType.DMA
    hidden, final = pl.pallas_call(
        functools.partial(kernel, n),
        out_shape=(
            pltpu.VMEM((atoms, ca), BF16),
            pltpu.VMEM((tokens + EXTRA, c), BF16),
        ),
        in_specs=[pl.BlockSpec(memory_space=pltpu.HBM)] * len(operands),
        out_specs=(pl.BlockSpec(memory_space=pltpu.VMEM),) * 2,
        scratch_shapes=[
            pltpu.VMEM((atoms + 2 * SIDE, ca), BF16),
            pltpu.VMEM((atoms + 2 * QW, AH * KW), BF16),
            pltpu.VMEM((1, atoms), jnp.int32),
            pltpu.VMEM((1, atoms), jnp.int32),
            pltpu.VMEM((1, atoms), jnp.int32),
            pltpu.VMEM((tokens + 2, all_tokens, cz), BF16),
            pltpu.VMEM(atom_qkv_w.shape, BF16),
            pltpu.VMEM(atom_out_w.shape, BF16),
            pltpu.VMEM(agg_w.shape, BF16),
            pltpu.VMEM(tok_qkv_w.shape, BF16),
            pltpu.VMEM(tok_out_w.shape, BF16),
            pltpu.VMEM(pair_w.shape[::-1], BF16),
            pltpu.VMEM((atoms + 2 * SIDE, 3 * ca), BF16),
            pltpu.VMEM((atoms + 2 * QW, ca), BF16),
            pltpu.VMEM((blocks, all_tokens, c), BF16),
            pltpu.VMEM((blocks, (tokens + 2) * H, all_tokens), BF16),
            dma((12,)),
            dma((8,)),
            dma((8,)),
            dma((blocks, n - 1)),
            dma((blocks, n - 1)),
        ],
        compiler_params=pltpu.CompilerParams(
            collective_id=0, has_side_effects=True, vmem_limit_bytes=56 * 1024 * 1024
        ),
    )(*operands)
    return pl.pallas_call(
        hand_over,
        out_shape=(
            jax.ShapeDtypeStruct((atoms, ca), BF16),
            jax.ShapeDtypeStruct((tokens, c), BF16),
        ),
    )(final, hidden, atom_token.reshape(1, atoms), bcast_w)


def solution(mesh):
    placed = (
        P(("seed", "tok"), None),
        P("tok", None),
        P("tok"),
        P("tok"),
        P("tok", None, None),
        P(),
        P(),
        P(),
        P(),
        P(),
        P(),
        P(),
    )
    return jax.shard_map(
        local,
        mesh=mesh,
        in_specs=placed,
        out_specs=(P(("seed", "tok"), None), P(("seed", "tok"), None)),
        check_vma=False,
    )
```

time: 92.2 us -> 29.5 us (0.32)
  the two profiles are of different devices: /device:TPU:28 before, /device:TPU:1 now
where the time goes in v1:
time: 29.5 us; the launch traced here: 29.4 us
  Pallas kernels  27.5 us (93%)
  local copies, waits for them, and re-layouts  1.23 us (4%)
  between operations  0.65 us (2%)
    pallas_call x1, Pallas kernels, local(): pl.pallas_call(functools.partial(kernel, n), out_shape=(pltpu.VMEM((atoms...  25.5 us
    pallas_call x1, Pallas kernels, local(): pl.pallas_call(hand_over, out_shape=(jax.ShapeDtypeStruct((atoms, ca), BF...  1.97 us
    unnamed x4, local copies, waits for them, and re-layouts  1.23 us

profile of v1, /device:TPU:1, one launch (start us, length us, event | category | flops | bytes accessed | tf_op | source)
XLA Modules:
  0.0 29.4 jit_solution(2072652689412784866)
XLA Ops:
  0.6 25.5 %shard_map.122 = (bf16[256,128]{1,0:T(8,128)(2,1)S(1)}, bf16[48,768]{1,0:T(8,128)(2,1)S(1)}) custom-call(bf16[256,128]{1,0:T(8,128)(2,1)} %single_hbm.1, bf16[256,512]{1,0:T(8,128)(2,1)} %bias_hbm.1, s32[1,256]{1,0:T(1,128)} %bitcast.3, bf16[32,256,128]{2,1,0:T(8,128)(2,1)} %pair_hbm.1, bf16[128,384]{1,0:T(8,128)(2,1)} %qkv_hbm.1, ...), custom_call_target="tpu_custom_call" | custom-call | tf_op jit(solution)/shard_map/pallas_call | solution.py:318
  26.2 0.0 copy-start
  26.2 0.6 %copy-done = bf16[48,768]{1,0:T(8,128)(2,1)} copy-done((bf16[48,768]{1,0:T(8,128)(2,1)}, bf16[48,768]{1,0:T(8,128)(2,1)S(1)}, u32[]{:S(2)}) %copy-start) | copy-done | bytes 73752
  26.8 0.0 copy-start.1
  26.8 0.6 %copy-done.1 = bf16[256,128]{1,0:T(8,128)(2,1)} copy-done((bf16[256,128]{1,0:T(8,128)(2,1)}, bf16[256,128]{1,0:T(8,128)(2,1)S(1)}, u32[]{:S(2)}) %copy-start.1) | copy-done | bytes 65560
  27.4 2.0 %shard_map.123 = (bf16[256,128]{1,0:T(8,128)(2,1)}, bf16[32,768]{1,0:T(8,128)(2,1)}) custom-call(bf16[48,768]{1,0:T(8,128)(2,1)} %copy-done, bf16[256,128]{1,0:T(8,128)(2,1)} %copy-done.1, s32[1,256]{1,0:T(1,128)} %bitcast.4, bf16[768,128]{1,0:T(8,128)(2,1)} %bcast.1), custom_call_target="tpu_custom_call" | custom-call | tf_op jit(solution)/shard_map/pallas_call | solution.py:353
Async XLA Ops:
  26.2 0.6 %copy-start = (bf16[48,768]{1,0:T(8,128)(2,1)}, bf16[48,768]{1,0:T(8,128)(2,1)S(1)}, u32[]{:S(2)}) copy-start(bf16[48,768]{1,0:T(8,128)(2,1)S(1)} %get-tuple-element.4.final) | copy-start | bytes 221188
  26.8 0.6 %copy-start.1 = (bf16[256,128]{1,0:T(8,128)(2,1)}, bf16[256,128]{1,0:T(8,128)(2,1)S(1)}, u32[]{:S(2)}) copy-start(bf16[256,128]{1,0:T(8,128)(2,1)S(1)} %get-tuple-element.5.hidden) | copy-start | bytes 196612

commit v2 on v1

--- a/solution.py
+++ b/solution.py
@@ -56,8 +56,9 @@
     tqkv_hbm,
     tout_hbm,
     pairw_hbm,
-    hidden_out,
-    final_out,
+    bcast_hbm,
+    atom_out,
+    token_out,
     xs,
     bs,
     tok_mid,
@@ -70,15 +71,19 @@
     tqkv_w,
     tout_w,
     pair_w,
+    bcast_w,
     proj,
     mixed,
     gathered,
+    keyvals,
     pbias,
     local_sem,
     halo_send,
     halo_recv,
     gather_send,
     gather_recv,
+    relay_send,
+    relay_recv,
 ):
     atoms, ca = single_hbm.shape
     tokens = pair_hbm.shape[0]
@@ -113,6 +118,7 @@
         (tout_hbm.at[0], tout_w.at[0]),
         (tqkv_hbm.at[1], tqkv_w.at[1]),
         (tout_hbm.at[1], tout_w.at[1]),
+        (bcast_hbm, bcast_w),
     ]
     copies = [
         pltpu.make_async_copy(src, dst, local_sem.at[i]) for i, (src, dst) in enumerate(moves)
@@ -122,6 +128,7 @@
     (c_single, c_bias, c_token, c_qkv, c_aout, c_agg, c_pairw, c_pair) = copies[:8]
     c_tqkv = [copies[8], copies[10]]
     c_tout = [copies[9], copies[11]]
+    c_bcast = copies[12]
 
     pl.semaphore_wait(barrier, n - 1)
     halo_moves = [
@@ -182,7 +189,7 @@
         scores = jnp.where(inside, scores, -1000000000.0)
         powers = jnp.exp(scores - jnp.max(scores, axis=-1, keepdims=True))
         total = jnp.sum(powers, axis=-1, keepdims=True)
-        heads = dot(powers.astype(BF16), values) / total
+        heads = dot(powers.astype(BF16), values) * (1.0 / total)
         out = heads[:QW] * head_masks[0]
         for h in range(1, AH):
             out = out + heads[h * QW : (h + 1) * QW] * head_masks[h]
@@ -205,7 +212,6 @@
     c_agg.wait()
     own_rows = xs[HALO : HALO + ext_atoms].astype(F32)
     hidden = (own_rows + dot(mixed[...], aout_w[...])).astype(BF16)
-    hidden_out[...] = hidden[QW : QW + atoms]
     lifted = jnp.maximum(dot(hidden, agg_w[...]), 0.0)
 
     wanted = wanted_tokens(tokens, ext_tokens)
@@ -233,55 +239,98 @@
     head_lane = lax.broadcasted_iota(jnp.int32, (H, c), 1) // head_size
     tok_mask = (head_row == head_lane).astype(F32).astype(BF16)
     tok_mask = jnp.concatenate([tok_mask] * used, axis=0)
-    own = pl.ds(pl.multiple_of(me * tokens, tokens), tokens)
+    def flipped(index, bits):
+        bit = 1
+        while bit <= bits:
+            if bits & bit:
+                index = index + bit * (1 - 2 * lax.rem(index // bit, 2))
+            bit *= 2
+        return index
+
+    def shard(index):
+        return pl.ds(pl.multiple_of(index * tokens, tokens), tokens)
+
+    def send(b, index, to, send_sem, recv_sem):
+        copy = pltpu.make_async_remote_copy(
+            src_ref=gathered.at[b, shard(index)],
+            dst_ref=gathered.at[b, shard(index)],
+            send_sem=send_sem,
+            recv_sem=recv_sem,
+            device_id={"tok": to},
+            device_id_type=pl.DeviceIdType.MESH,
+        )
+        copy.start()
+        return copy
+
+    def project_keyvals(b, indices):
+        some = jnp.concatenate([gathered[b, shard(i), :] for i in indices], axis=0)
+        result = dot(some, tqkv_w[b, :, c:]).astype(BF16)
+        for k, i in enumerate(indices):
+            keyvals[shard(i), :] = result[k * tokens : (k + 1) * tokens]
+
+    chips = n // 2
+    mate = flipped(me, 1)
+    peers = [flipped(me, 2 * j) for j in range(chips)]
+    mate_peers = [flipped(mate, 2 * j) for j in range(chips)]
     for b in range(blocks):
         normed = layer_norm(stream).astype(BF16)
-        gathered[b, own, :] = normed[:tokens]
-        sends = [
-            pltpu.make_async_remote_copy(
-                src_ref=gathered.at[b, own],
-                dst_ref=gathered.at[b, own],
-                send_sem=gather_send.at[b, k - 1],
-                recv_sem=gather_recv.at[b, k - 1],
-                device_id={"tok": lax.rem(me + k, n)},
-                device_id_type=pl.DeviceIdType.MESH,
-            )
-            for k in range(1, n)
+        gathered[b, shard(me), :] = normed[:tokens]
+        direct = [
+            send(b, me, peers[j], gather_send.at[b, j - 1], gather_recv.at[b, j - 1])
+            for j in range(1, chips)
         ]
-        for copy in sends:
-            copy.start()
+        relays = [send(b, me, mate, relay_send.at[b, 0], relay_recv.at[b, 0])]
+
+        def relay(j):
+            direct[j - 1].wait_recv()
+            relays.append(send(b, peers[j], mate, relay_send.at[b, j], relay_recv.at[b, j]))
+
+        def queries():
+            c_tqkv[b].wait()
+            q = dot(normed, tqkv_w[b, :, :c]).astype(BF16)
+            return dot(spreader, q).astype(BF16) * tok_mask
+
         if b == 0:
             c_pairw.wait()
             c_pair.wait()
             for copy in halos[6:]:
                 copy.wait()
-            for t in range(used):
+            for t in range(used // 2):
                 pair_rows(t)
-        c_tqkv[b].wait()
-        q = dot(normed, tqkv_w[b, :, :c]).astype(BF16)
-        spread = dot(spreader, q).astype(BF16) * tok_mask
+            for j in range(1, chips - 1):
+                relay(j)
+            for t in range(used // 2, used):
+                pair_rows(t)
+            relay(chips - 1)
+            spread = queries()
+            relays[0].wait_recv()
+            project_keyvals(b, peers[: chips - 1] + mate_peers[:1])
+        else:
+            spread = queries()
+            for j in range(1, chips - 1):
+                relay(j)
+            relays[0].wait_recv()
+            project_keyvals(b, peers[: chips - 1] + mate_peers[:1])
+            relay(chips - 1)
+        for copy in relays[1:]:
+            copy.wait_recv()
+        project_keyvals(b, peers[chips - 1 :] + mate_peers[1:])
+        for copy in direct + relays:
+            copy.wait_send()
         c_tout[b].wait()
-        for copy in sends:
-            copy.wait()
-        everyone = gathered[b]
-        keys = dot(everyone, tqkv_w[b, :, c : 2 * c]).astype(BF16)
-        scores = dot_nt(spread, keys) * head_size ** (-0.5) + pbias[b].astype(F32)
+        scores = dot_nt(spread, keyvals[:, :c]) * head_size ** (-0.5) + pbias[b].astype(F32)
         powers = jnp.exp(scores - jnp.max(scores, axis=-1, keepdims=True))
         total = jnp.sum(powers, axis=-1, keepdims=True)
-        values = dot(everyone, tqkv_w[b, :, 2 * c :]).astype(BF16)
-        heads = (dot(powers.astype(BF16), values) / total).astype(BF16) * tok_mask
-        mixed = dot(collector, heads).astype(BF16)
-        stream = stream + dot(mixed, tout_w[b])
-
-    final_out[...] = stream.astype(BF16)
-
-
-def hand_over(final, hidden, token, bcast, atom_out, token_out):
-    tokens = token_out.shape[0]
-    token_out[...] = final[:tokens, :]
-    carry = dot(final[...], bcast[...]).astype(BF16)
-    mine = (token[...] == wanted_tokens(tokens, final.shape[0])).astype(F32).astype(BF16)
-    atom_out[...] = (hidden[...].astype(F32) + dot_tn(mine, carry)).astype(BF16)
+        heads = dot(powers.astype(BF16), keyvals[:, c:]) * (1.0 / total)
+        update = dot(collector, heads.astype(BF16) * tok_mask).astype(BF16)
+        stream = stream + dot(update, tout_w[b])
+
+    final = stream.astype(BF16)
+    token_out[...] = final[:tokens]
+    c_bcast.wait()
+    carry = dot(final, bcast_w[...]).astype(BF16)
+    mine = (tok_mid[...] == wanted).astype(F32).astype(BF16)
+    atom_out[...] = (hidden[QW : QW + atoms].astype(F32) + dot_tn(mine, carry)).astype(BF16)
 
 
 def local(
@@ -313,13 +362,14 @@
         tok_qkv_w,
         tok_out_w,
         pair_w.T,
+        bcast_w,
     )
     dma = pltpu.SemaphoreType.DMA
-    hidden, final = pl.pallas_call(
+    return pl.pallas_call(
         functools.partial(kernel, n),
         out_shape=(
             pltpu.VMEM((atoms, ca), BF16),
-            pltpu.VMEM((tokens + EXTRA, c), BF16),
+            pltpu.VMEM((tokens, c), BF16),
         ),
         in_specs=[pl.BlockSpec(memory_space=pltpu.HBM)] * len(operands),
         out_specs=(pl.BlockSpec(memory_space=pltpu.VMEM),) * 2,
@@ -336,27 +386,24 @@
             pltpu.VMEM(tok_qkv_w.shape, BF16),
             pltpu.VMEM(tok_out_w.shape, BF16),
             pltpu.VMEM(pair_w.shape[::-1], BF16),
+            pltpu.VMEM(bcast_w.shape, BF16),
             pltpu.VMEM((atoms + 2 * SIDE, 3 * ca), BF16),
             pltpu.VMEM((atoms + 2 * QW, ca), BF16),
             pltpu.VMEM((blocks, all_tokens, c), BF16),
+            pltpu.VMEM((all_tokens, 2 * c), BF16),
             pltpu.VMEM((blocks, (tokens + 2) * H, all_tokens), BF16),
-            dma((12,)),
+            dma((13,)),
             dma((8,)),
             dma((8,)),
-            dma((blocks, n - 1)),
-            dma((blocks, n - 1)),
+            dma((blocks, n // 2 - 1)),
+            dma((blocks, n // 2 - 1)),
+            dma((blocks, n // 2)),
+            dma((blocks, n // 2)),
         ],
         compiler_params=pltpu.CompilerParams(
             collective_id=0, has_side_effects=True, vmem_limit_bytes=56 * 1024 * 1024
         ),
     )(*operands)
-    return pl.pallas_call(
-        hand_over,
-        out_shape=(
-            jax.ShapeDtypeStruct((atoms, ca), BF16),
-            jax.ShapeDtypeStruct((tokens, c), BF16),
-        ),
-    )(final, hidden, atom_token.reshape(1, atoms), bcast_w)
 
 
 def solution(mesh):

time: 29.5 us -> 27.9 us (0.946)
  Pallas kernels: 27.5 us -> 25.9 us
    pallas_call x1 -> x0, Pallas kernels: 1.97 us -> none  [local(): pl.pallas_call(hand_over, out_shape=(jax.ShapeDtypeStruct((atoms, ca), BF...]
    pallas_call x1, Pallas kernels: 25.5 us -> 25.9 us  [local(): pl.pallas_call(functools.partial(kernel, n), out_shape=(pltpu.VMEM((atoms...]
    unnamed x4 -> x2, local copies, waits for them, and re-layouts: 1.23 us -> 1.25 us
where the time goes in v2:
time: 27.9 us; the launch traced here: 27.8 us
  Pallas kernels  25.9 us (93%)
  local copies, waits for them, and re-layouts  1.25 us (4%)
  between operations  0.64 us (2%)
    pallas_call x1, Pallas kernels, local(): pl.pallas_call(functools.partial(kernel, n), out_shape=(pltpu.VMEM((atoms...  25.9 us
    unnamed x2, local copies, waits for them, and re-layouts  1.25 us

profile of v2, /device:TPU:1, one launch (start us, length us, event | category | flops | bytes accessed | tf_op | source)
XLA Modules:
  0.0 27.8 jit_solution(7054568494066388513)
XLA Ops:
  0.6 25.9 %shard_map.122 = (bf16[256,128]{1,0:T(8,128)(2,1)S(1)}, bf16[32,768]{1,0:T(8,128)(2,1)S(1)}) custom-call(bf16[256,128]{1,0:T(8,128)(2,1)} %single_hbm.1, bf16[256,512]{1,0:T(8,128)(2,1)} %bias_hbm.1, s32[1,256]{1,0:T(1,128)} %bitcast.3, bf16[32,256,128]{2,1,0:T(8,128)(2,1)} %pair_hbm.1, bf16[128,384]{1,0:T(8,128)(2,1)} %qkv_hbm.1, ...), custom_call_target="tpu_custom_call" | custom-call | tf_op jit(solution)/shard_map/pallas_call | solution.py:368
  26.5 0.6 %copy.15 = bf16[256,128]{1,0:T(8,128)(2,1)} copy(bf16[256,128]{1,0:T(8,128)(2,1)S(1)} %get-tuple-element.2) | data formatting | bytes 131072
  27.2 0.6 %copy.16 = bf16[32,768]{1,0:T(8,128)(2,1)} copy(bf16[32,768]{1,0:T(8,128)(2,1)S(1)} %get-tuple-element.3) | data formatting | bytes 98304

commit v3 on v2

--- a/solution.py
+++ b/solution.py
@@ -130,6 +130,39 @@
     c_tout = [copies[9], copies[11]]
     c_bcast = copies[12]
 
+    def flipped(index, bits):
+        bit = 1
+        while bit <= bits:
+            if bits & bit:
+                index = index + bit * (1 - 2 * lax.rem(lax.div(index, bit), 2))
+            bit *= 2
+        return index
+
+    chips = n // 2
+    mate = flipped(me, 1)
+    peers = [flipped(me, 2 * j) for j in range(chips)]
+    mate_peers = [flipped(mate, 2 * j) for j in range(chips)]
+
+    def between(shape, dim, size):
+        offset = lax.broadcasted_iota(jnp.int32, shape, 1 - dim) - size * lax.broadcasted_iota(
+            jnp.int32, shape, dim
+        )
+        return ((offset >= 0) & (offset < size)).astype(F32)
+
+    width = ca // AH
+    rows = used * H
+    head_size = c // H
+    lane = lax.broadcasted_iota(jnp.int32, (QW, ca), 1)
+    head_masks = [
+        ((lane >= width * h) & (lane < width * (h + 1))).astype(F32) for h in range(AH)
+    ]
+    head_picks = [m.astype(BF16) for m in head_masks]
+    key_lane = lax.broadcasted_iota(jnp.int32, (1, KW), 1)
+    spreader = between((rows, ext_tokens), 1, H).astype(BF16)
+    collector = between((ext_tokens, rows), 0, H).astype(BF16)
+    tok_mask = between((H, c), 0, head_size).astype(BF16)
+    tok_mask = jnp.concatenate([tok_mask] * used, axis=0)
+
     pl.semaphore_wait(barrier, n - 1)
     halo_moves = [
         (single_hbm.at[atoms - SIDE : atoms], xs.at[0:SIDE], right),
@@ -158,56 +191,70 @@
         copy.start()
 
     def pair_rows(t):
-        rows = dot_nt(pair_w[...], pair[t]).astype(BF16)
-        for b in range(blocks):
-            pbias[b, t * H : (t + 1) * H, :] = rows[b * H : (b + 1) * H]
+        weight = pair_w[...]
+        blank = jnp.zeros_like(weight)
+        both = jnp.concatenate(
+            [
+                jnp.concatenate([weight, blank], axis=1),
+                jnp.concatenate([blank, weight], axis=1),
+            ],
+            axis=0,
+        )
+        duo = jnp.concatenate([pair[t], pair[t + 1]], axis=1)
+        rows = dot_nt(both, duo).astype(BF16)
+        for k in range(2):
+            for b in range(blocks):
+                at = (k * blocks + b) * H
+                pbias[b, (t + k) * H : (t + k + 1) * H, :] = rows[at : at + H]
 
     c_single.wait()
     c_bias.wait()
     c_token.wait()
     c_qkv.wait()
-    width = ca // AH
-    lane = lax.broadcasted_iota(jnp.int32, (QW, ca), 1)
-    head_masks = [(lane // width == h).astype(F32) for h in range(AH)]
-    head_picks = [m.astype(BF16) for m in head_masks]
-    key_lane = lax.broadcasted_iota(jnp.int32, (1, KW), 1)
 
     def project(rows):
         return dot(layer_norm(rows.astype(F32)).astype(BF16), qkv_w[...]).astype(BF16)
 
-    def window(w):
-        q = proj[HALO + QW * w : HALO + QW * (w + 1), :ca]
-        keys = proj[QW * w : QW * w + KW, ca : 2 * ca]
-        values = proj[QW * w : QW * w + KW, 2 * ca :]
-        spread = jnp.concatenate([q * pick for pick in head_picks], axis=0)
-        bias = jnp.concatenate(
-            [bs[QW * w : QW * (w + 1), h * KW : (h + 1) * KW] for h in range(AH)], axis=0
-        )
-        scores = dot_nt(spread, keys) * width ** (-0.5) + bias.astype(F32)
-        position = me * atoms - SIDE + QW * w + key_lane
-        inside = (position >= 0) & (position < n * atoms)
-        scores = jnp.where(inside, scores, -1000000000.0)
-        powers = jnp.exp(scores - jnp.max(scores, axis=-1, keepdims=True))
-        total = jnp.sum(powers, axis=-1, keepdims=True)
-        heads = dot(powers.astype(BF16), values) * (1.0 / total)
-        out = heads[:QW] * head_masks[0]
-        for h in range(1, AH):
-            out = out + heads[h * QW : (h + 1) * QW] * head_masks[h]
-        mixed[QW * w : QW * (w + 1), :] = out.astype(BF16)
+    def attend(some, masked):
+        scores = []
+        for w in some:
+            q = proj[HALO + QW * w : HALO + QW * (w + 1), :ca]
+            keys = proj[QW * w : QW * w + KW, ca : 2 * ca]
+            spread = jnp.concatenate([q * pick for pick in head_picks], axis=0)
+            scores.append(dot_nt(spread, keys))
+        for i, w in enumerate(some):
+            bias = jnp.concatenate(
+                [bs[QW * w : QW * (w + 1), h * KW : (h + 1) * KW] for h in range(AH)], axis=0
+            )
+            scores[i] = scores[i] * width ** (-0.5) + bias.astype(F32)
+            if masked:
+                position = me * atoms - SIDE + QW * w + key_lane
+                inside = (position >= 0) & (position < n * atoms)
+                scores[i] = jnp.where(inside, scores[i], -1000000000.0)
+        maxima = [jnp.max(x, axis=-1, keepdims=True) for x in scores]
+        powers = [jnp.exp(x - m) for x, m in zip(scores, maxima)]
+        totals = [jnp.sum(x, axis=-1, keepdims=True) for x in powers]
+        heads = [
+            dot(x.astype(BF16), proj[QW * w : QW * w + KW, 2 * ca :])
+            for w, x in zip(some, powers)
+        ]
+        for w, x, total in zip(some, heads, totals):
+            x = x * (1.0 / total)
+            out = x[:QW] * head_masks[0]
+            for h in range(1, AH):
+                out = out + x[h * QW : (h + 1) * QW] * head_masks[h]
+            mixed[QW * w : QW * (w + 1), :] = out.astype(BF16)
 
     windows = range(ext_atoms // QW)
     inner = [w for w in windows if QW * w >= SIDE and QW * w + KW <= SIDE + atoms]
     proj[SIDE : SIDE + atoms, :] = project(xs[SIDE : SIDE + atoms])
-    for w in inner:
-        window(w)
+    attend(inner, False)
     for copy in halos[:6]:
         copy.wait()
     edges = project(jnp.concatenate([xs[:SIDE], xs[SIDE + atoms :]], axis=0))
     proj[:SIDE, :] = edges[:SIDE]
     proj[SIDE + atoms :, :] = edges[SIDE:]
-    for w in windows:
-        if w not in inner:
-            window(w)
+    attend([w for w in windows if w not in inner], True)
     c_aout.wait()
     c_agg.wait()
     own_rows = xs[HALO : HALO + ext_atoms].astype(F32)
@@ -224,28 +271,6 @@
     upper = lifted.astype(BF16)
     lower = (lifted - upper.astype(F32)).astype(BF16)
     stream = (dot(picker, upper) + dot(picker, lower)) / count
-
-    rows = used * H
-    head_size = c // H
-    row_token = lax.broadcasted_iota(jnp.int32, (rows, ext_tokens), 0) // H
-    spreader = (row_token == lax.broadcasted_iota(jnp.int32, (rows, ext_tokens), 1)).astype(
-        F32
-    ).astype(BF16)
-    col_token = lax.broadcasted_iota(jnp.int32, (ext_tokens, rows), 1) // H
-    collector = (col_token == lax.broadcasted_iota(jnp.int32, (ext_tokens, rows), 0)).astype(
-        F32
-    ).astype(BF16)
-    head_row = lax.broadcasted_iota(jnp.int32, (H, c), 0)
-    head_lane = lax.broadcasted_iota(jnp.int32, (H, c), 1) // head_size
-    tok_mask = (head_row == head_lane).astype(F32).astype(BF16)
-    tok_mask = jnp.concatenate([tok_mask] * used, axis=0)
-    def flipped(index, bits):
-        bit = 1
-        while bit <= bits:
-            if bits & bit:
-                index = index + bit * (1 - 2 * lax.rem(index // bit, 2))
-            bit *= 2
-        return index
 
     def shard(index):
         return pl.ds(pl.multiple_of(index * tokens, tokens), tokens)
@@ -268,10 +293,6 @@
         for k, i in enumerate(indices):
             keyvals[shard(i), :] = result[k * tokens : (k + 1) * tokens]
 
-    chips = n // 2
-    mate = flipped(me, 1)
-    peers = [flipped(me, 2 * j) for j in range(chips)]
-    mate_peers = [flipped(mate, 2 * j) for j in range(chips)]
     for b in range(blocks):
         normed = layer_norm(stream).astype(BF16)
         gathered[b, shard(me), :] = normed[:tokens]
@@ -295,11 +316,12 @@
             c_pair.wait()
             for copy in halos[6:]:
                 copy.wait()
-            for t in range(used // 2):
+            half = used // 4 * 2
+            for t in range(0, half, 2):
                 pair_rows(t)
             for j in range(1, chips - 1):
                 relay(j)
-            for t in range(used // 2, used):
+            for t in range(half, used, 2):
                 pair_rows(t)
             relay(chips - 1)
             spread = queries()

time: 27.9 us -> 27 us (0.968)
  Pallas kernels: 25.9 us -> 25 us
    pallas_call x1, Pallas kernels: 25.9 us -> 25 us  [local(): pl.pallas_call(functools.partial(kernel, n), out_shape=(pltpu.VMEM((atoms...]
where the time goes in v3:
time: 27 us; the launch traced here: 26.9 us
  Pallas kernels  25 us (93%)
  local copies, waits for them, and re-layouts  1.25 us (5%)
  between operations  0.64 us (2%)
    pallas_call x1, Pallas kernels, local(): pl.pallas_call(functools.partial(kernel, n), out_shape=(pltpu.VMEM((atoms...  25 us
    unnamed x2, local copies, waits for them, and re-layouts  1.25 us

profile of v3, /device:TPU:1, one launch (start us, length us, event | category | flops | bytes accessed | tf_op | source)
XLA Modules:
  0.0 26.9 jit_solution(14406462879067549349)
XLA Ops:
  0.6 25.0 %shard_map.122 = (bf16[256,128]{1,0:T(8,128)(2,1)S(1)}, bf16[32,768]{1,0:T(8,128)(2,1)S(1)}) custom-call(bf16[256,128]{1,0:T(8,128)(2,1)} %single_hbm.1, bf16[256,512]{1,0:T(8,128)(2,1)} %bias_hbm.1, s32[1,256]{1,0:T(1,128)} %bitcast.3, bf16[32,256,128]{2,1,0:T(8,128)(2,1)} %pair_hbm.1, bf16[128,384]{1,0:T(8,128)(2,1)} %qkv_hbm.1, ...), custom_call_target="tpu_custom_call" | custom-call | tf_op jit(solution)/shard_map/pallas_call | solution.py:390
  25.6 0.6 %copy.15 = bf16[256,128]{1,0:T(8,128)(2,1)} copy(bf16[256,128]{1,0:T(8,128)(2,1)S(1)} %get-tuple-element.2) | data formatting | bytes 131072
  26.2 0.6 %copy.16 = bf16[32,768]{1,0:T(8,128)(2,1)} copy(bf16[32,768]{1,0:T(8,128)(2,1)S(1)} %get-tuple-element.3) | data formatting | bytes 98304

commit v4 on v3

--- a/solution.py
+++ b/solution.py
@@ -75,7 +75,6 @@
     proj,
     mixed,
     gathered,
-    keyvals,
     pbias,
     local_sem,
     halo_send,
@@ -141,7 +140,6 @@
     chips = n // 2
     mate = flipped(me, 1)
     peers = [flipped(me, 2 * j) for j in range(chips)]
-    mate_peers = [flipped(mate, 2 * j) for j in range(chips)]
 
     def between(shape, dim, size):
         offset = lax.broadcasted_iota(jnp.int32, shape, 1 - dim) - size * lax.broadcasted_iota(
@@ -287,12 +285,6 @@
         copy.start()
         return copy
 
-    def project_keyvals(b, indices):
-        some = jnp.concatenate([gathered[b, shard(i), :] for i in indices], axis=0)
-        result = dot(some, tqkv_w[b, :, c:]).astype(BF16)
-        for k, i in enumerate(indices):
-            keyvals[shard(i), :] = result[k * tokens : (k + 1) * tokens]
-
     for b in range(blocks):
         normed = layer_norm(stream).astype(BF16)
         gathered[b, shard(me), :] = normed[:tokens]
@@ -325,27 +317,24 @@
                 pair_rows(t)
             relay(chips - 1)
             spread = queries()
-            relays[0].wait_recv()
-            project_keyvals(b, peers[: chips - 1] + mate_peers[:1])
         else:
             spread = queries()
-            for j in range(1, chips - 1):
+            for j in range(1, chips):
                 relay(j)
-            relays[0].wait_recv()
-            project_keyvals(b, peers[: chips - 1] + mate_peers[:1])
-            relay(chips - 1)
-        for copy in relays[1:]:
+        for copy in relays:
             copy.wait_recv()
-        project_keyvals(b, peers[chips - 1 :] + mate_peers[1:])
+        c_tout[b].wait()
+        everyone = gathered[b]
+        keys = dot(everyone, tqkv_w[b, :, c : 2 * c]).astype(BF16)
+        scores = dot_nt(spread, keys) * head_size ** (-0.5) + pbias[b].astype(F32)
+        powers = jnp.exp(scores - jnp.max(scores, axis=-1, keepdims=True))
+        total = jnp.sum(powers, axis=-1, keepdims=True)
+        values = dot(everyone, tqkv_w[b, :, 2 * c :]).astype(BF16)
+        heads = dot(powers.astype(BF16), values) * (1.0 / total)
+        update = dot(collector, heads.astype(BF16) * tok_mask).astype(BF16)
+        stream = stream + dot(update, tout_w[b])
         for copy in direct + relays:
             copy.wait_send()
-        c_tout[b].wait()
-        scores = dot_nt(spread, keyvals[:, :c]) * head_size ** (-0.5) + pbias[b].astype(F32)
-        powers = jnp.exp(scores - jnp.max(scores, axis=-1, keepdims=True))
-        total = jnp.sum(powers, axis=-1, keepdims=True)
-        heads = dot(powers.astype(BF16), keyvals[:, c:]) * (1.0 / total)
-        update = dot(collector, heads.astype(BF16) * tok_mask).astype(BF16)
-        stream = stream + dot(update, tout_w[b])
 
     final = stream.astype(BF16)
     token_out[...] = final[:tokens]
@@ -412,7 +401,6 @@
             pltpu.VMEM((atoms + 2 * SIDE, 3 * ca), BF16),
             pltpu.VMEM((atoms + 2 * QW, ca), BF16),
             pltpu.VMEM((blocks, all_tokens, c), BF16),
-            pltpu.VMEM((all_tokens, 2 * c), BF16),
             pltpu.VMEM((blocks, (tokens + 2) * H, all_tokens), BF16),
             dma((13,)),
             dma((8,)),

time: 27 us -> 26.1 us (0.967)
  Pallas kernels: 25 us -> 24.1 us
    pallas_call x1, Pallas kernels: 25 us -> 24.1 us  [local(): pl.pallas_call(functools.partial(kernel, n), out_shape=(pltpu.VMEM((atoms...]
where the time goes in v4:
time: 26.1 us; the launch traced here: 26 us
  Pallas kernels  24.1 us (92%)
  local copies, waits for them, and re-layouts  1.25 us (5%)
  between operations  0.64 us (2%)
    pallas_call x1, Pallas kernels, local(): pl.pallas_call(functools.partial(kernel, n), out_shape=(pltpu.VMEM((atoms...  24.1 us
    unnamed x2, local copies, waits for them, and re-layouts  1.25 us

profile of v4, /device:TPU:1, one launch (start us, length us, event | category | flops | bytes accessed | tf_op | source)
XLA Modules:
  0.0 26.0 jit_solution(9527643618592069876)
XLA Ops:
  0.6 24.1 %shard_map.122 = (bf16[256,128]{1,0:T(8,128)(2,1)S(1)}, bf16[32,768]{1,0:T(8,128)(2,1)S(1)}) custom-call(bf16[256,128]{1,0:T(8,128)(2,1)} %single_hbm.1, bf16[256,512]{1,0:T(8,128)(2,1)} %bias_hbm.1, s32[1,256]{1,0:T(1,128)} %bitcast.3, bf16[32,256,128]{2,1,0:T(8,128)(2,1)} %pair_hbm.1, bf16[128,384]{1,0:T(8,128)(2,1)} %qkv_hbm.1, ...), custom_call_target="tpu_custom_call" | custom-call | tf_op jit(solution)/shard_map/pallas_call | solution.py:379
  24.7 0.6 %copy.15 = bf16[256,128]{1,0:T(8,128)(2,1)} copy(bf16[256,128]{1,0:T(8,128)(2,1)S(1)} %get-tuple-element.2) | data formatting | bytes 131072
  25.4 0.6 %copy.16 = bf16[32,768]{1,0:T(8,128)(2,1)} copy(bf16[32,768]{1,0:T(8,128)(2,1)S(1)} %get-tuple-element.3) | data formatting | bytes 98304
